TPU v7x, 32 devices: a whole 2x2x4 slice. The times are simulated.
32 devices in a mesh: seq: 8 (over z, core), tp: 4 (over y, x).
Axes of the slice: x: 2, y: 2, z: 4, core: 2. Of those that a mesh axis runs over, the one named last changes fastest.
Arguments:
- trainer_rows: float32 [2, 1024, 12544], P(None, ('seq', 'tp')), as said below
- shard_order: int32 [32], replicated, may hold values from 0 to 31, each once
- residual_in: float32 [8192, 1024], P(('seq', 'tp')), may hold values from -6 to 6
- norm_gains: float32 [2, 2, 1024], replicated, may hold values from 0.25 to 1.75
- prompt_lengths: int32 [8, 4], P('seq'), may hold values from 1 to 512, 1024 in all within a row
- variate_ids: int32 [8192], P('seq'), may hold values from 0 to 7
- variate_bias: float32 [2, 16, 2], replicated, may hold values from -2 to 260
Outputs:
- hidden_states: float32 [8192, 1024], P(('seq', 'tp'))
Inputs may be any that keep to these rules, and one draw needn't show every extreme that they name: shard_order is a permutation of the trainer shards' row blocks. `prompt_lengths`: each row sums to 1024, and one entry of each row is 512. `trainer_rows`: entries of columns up to 9728 are at most 6 / sqrt(1024) in size, later ones at most 6 / sqrt(2816).
All inputs are finite; a program needn't handle non-finite values.
Results may differ from a plain program's by a relative error of at most 0.017.
Values may be sent and summed in bfloat16 or wider, within the bound.
A program may use at most 128 MiB of HBM per device.

v0:
```python
import jax
import jax.numpy as jnp
from jax import lax
from jax.sharding import PartitionSpec as P

NEGATIVE = -1e30
EPSILON = 1e-05


def rms_scaled(values, gain):
    mean_square = jnp.mean(values * values, axis=-1, keepdims=True)
    return values * lax.rsqrt(mean_square + EPSILON) * gain


def rotate(values, offsets):
    half_width = values.shape[-1] // 2
    frequency = 10000.0 ** (-jnp.arange(half_width, dtype=jnp.float32) / half_width)
    angles = offsets.astype(jnp.float32)[:, None] * frequency[None, :]
    cosine = jnp.cos(angles)[:, None, :]
    sine_part = jnp.sin(angles)[:, None, :]
    front_half = values[..., :half_width]
    back_half = values[..., half_width:]
    return jnp.concatenate(
        [front_half * cosine - back_half * sine_part, front_half * sine_part + back_half * cosine],
        axis=-1,
    )


def prompt_layout(lengths, token_count):
    prompt_ends = jnp.cumsum(lengths)
    prompt_starts = prompt_ends - lengths
    positions = jnp.arange(token_count, dtype=jnp.int32)
    segment = jnp.sum((positions[:, None] >= prompt_ends[None, :]).astype(jnp.int32), axis=1)
    member = segment[:, None] == jnp.arange(lengths.shape[0], dtype=jnp.int32)[None, :]
    offsets = positions - jnp.sum(jnp.where(member, prompt_starts[None, :], 0), axis=1)
    return (segment, offsets)


def project_rows(row_piece, weight):
    return jnp.dot(row_piece, weight, preferred_element_type=jnp.float32)


def gated_units(row_piece, weight):
    gate_up = jnp.dot(row_piece, weight, preferred_element_type=jnp.float32)
    half_width = weight.shape[1] // 2
    return (jax.nn.silu(gate_up[:, :half_width]) * gate_up[:, half_width:]).astype(jnp.bfloat16)


def project_out(source, weight):
    return lax.dot_general(
        source, weight, (((1,), (1,)), ((), ())), preferred_element_type=jnp.float32
    )


def on_device(
    trainer_rows, shard_order, residual_in, norm_gains, prompt_lengths, variate_ids, variate_bias
):
    tp_count = lax.axis_size("tp")
    seq_count = lax.axis_size("seq")
    layer_count, block_rows, total_cols = trainer_rows.shape
    model_width = residual_in.shape[1]
    ff_width = (total_cols - 4 * model_width) // 3
    head_cols = model_width // tp_count
    unit_cols = ff_width // tp_count
    rounded = trainer_rows.astype(jnp.bfloat16)
    part_widths = [model_width] * 4 + [ff_width] * 3
    grouped_parts = []
    column_start = 0
    for part_width in part_widths:
        grouped_parts.append(
            rounded[:, :, column_start : column_start + part_width].reshape(
                layer_count, block_rows, tp_count, part_width // tp_count
            )
        )
        column_start = column_start + part_width
    grouped = jnp.concatenate(grouped_parts, axis=3)
    slot_index = jnp.arange(seq_count * tp_count, dtype=jnp.int32)
    regrouped = lax.all_to_all(grouped, "tp", split_axis=2, concat_axis=1, tiled=True)
    collected = lax.all_gather(regrouped, "seq", axis=1, tiled=True)
    local_cols = collected.shape[3]
    blocks = collected.reshape(layer_count, seq_count * tp_count, block_rows, local_cols)
    placed = jnp.zeros_like(blocks).at[:, shard_order[slot_index]].set(blocks)
    weights = placed.reshape(layer_count, model_width, local_cols)
    token_count = variate_ids.shape[0]
    segment, offsets = prompt_layout(prompt_lengths[0], token_count)
    same_prompt = segment[:, None] == segment[None, :]
    same_variate = variate_ids[:, None] == variate_ids[None, :]
    head_count = variate_bias.shape[1]
    local_heads = head_count // tp_count
    head_size = head_cols // local_heads
    bias_table = lax.dynamic_slice_in_dim(
        variate_bias, lax.axis_index("tp") * local_heads, local_heads, 1
    )
    residual = residual_in
    for layer_index in range(layer_count):
        layer_bias = bias_table[layer_index]
        pair_bias = jnp.where(
            same_variate[None], layer_bias[:, 1][:, None, None], layer_bias[:, 0][:, None, None]
        )
        layer_weights = weights[layer_index]
        qkv_weight = layer_weights[:, : 3 * head_cols]
        out_weight = layer_weights[:, 3 * head_cols : 4 * head_cols]
        gate_up_weight = layer_weights[:, 4 * head_cols : 4 * head_cols + 2 * unit_cols]
        down_weight = layer_weights[:, 4 * head_cols + 2 * unit_cols :]
        normed = rms_scaled(residual, norm_gains[layer_index, 0]).astype(jnp.bfloat16)
        projected = project_rows(
            lax.all_gather(normed, "tp", axis=0, tiled=True), weight=qkv_weight
        )
        queries = rotate(
            projected[:, :head_cols].reshape(token_count, local_heads, head_size), offsets
        ).astype(jnp.bfloat16)
        key_rows = rotate(
            projected[:, head_cols : 2 * head_cols].reshape(token_count, local_heads, head_size),
            offsets,
        ).astype(jnp.bfloat16)
        values = (
            projected[:, 2 * head_cols : 3 * head_cols]
            .reshape(token_count, local_heads, head_size)
            .astype(jnp.bfloat16)
        )
        scores = (
            jnp.einsum("qhd,khd->hqk", queries, key_rows, preferred_element_type=jnp.float32)
            * head_size ** (-0.5)
            + pair_bias
        )
        scores = jnp.where(same_prompt[None], scores, NEGATIVE)
        row_peak = jnp.max(scores, axis=2, keepdims=True)
        weights_exp = jnp.exp(scores - row_peak)
        attn_weights = (weights_exp / jnp.sum(weights_exp, axis=2, keepdims=True)).astype(
            jnp.bfloat16
        )
        mixed_heads = (
            jnp.einsum("hqk,khd->qhd", attn_weights, values, preferred_element_type=jnp.float32)
            .astype(jnp.bfloat16)
            .reshape(token_count, head_cols)
        )
        head_total = lax.psum_scatter(
            project_out(source=mixed_heads, weight=out_weight).astype(jnp.bfloat16),
            "tp",
            scatter_dimension=0,
            tiled=True,
        ).astype(jnp.float32)
        residual = residual + head_total
        normed_mlp = rms_scaled(residual, norm_gains[layer_index, 1]).astype(jnp.bfloat16)
        hidden = gated_units(
            lax.all_gather(normed_mlp, "tp", axis=0, tiled=True), weight=gate_up_weight
        )
        unit_total = lax.psum_scatter(
            project_out(source=hidden, weight=down_weight).astype(jnp.bfloat16),
            "tp",
            scatter_dimension=0,
            tiled=True,
        ).astype(jnp.float32)
        residual = residual + unit_total
    return residual


def solution(mesh):
    return jax.shard_map(
        on_device,
        mesh=mesh,
        in_specs=(
            P(None, ("seq", "tp"), None),
            P(),
            P(("seq", "tp"), None),
            P(),
            P("seq", None),
            P("seq"),
            P(),
        ),
        out_specs=P(("seq", "tp"), None),
        check_vma=False,
    )
```

profile of v0, /device:TPU:0, one launch (start us, length us, event | category | flops | bytes accessed | tf_op | source)
XLA Modules:
  0.0 569.4 jit_solution(459971261398150591)
XLA Ops:
  6.5 2.1 convert_element_type.89
  8.6 0.1 fusion.76
  8.7 0.1 fusion.75
  8.8 0.1 reshape.232
  8.9 0.1 reshape.233
  8.9 0.1 reshape.234
  9.0 0.1 reshape.235
  9.1 0.5 reshape.236
  9.6 0.5 reshape.237
  10.0 0.5 reshape.238
  10.5 4.0 concatenate.19
  14.5 0.2 copy.38
  14.7 25.7 %all_to_all.18 = bf16[2,32,4,3136]{3,1,0,2:T(8,128)(2,1)S(1)} all-to-all(bf16[2,32,4,3136]{3,1,0,2:T(8,128)(2,1)S(1)} %copy.38), channel_id=1, replica_groups=mesh['seq'=8,'tp'=4] {'tp'}, dimensions={2} | all-to-all | bytes 3211264 | tf_op jit(solution)/shard_map/all_to_all | solution.py:78
  40.4 1.3 copy.39
  41.7 0.0 all-gather.6.cloned.1.call-start
  41.8 0.1 multiply_reduce_fusion.3
  42.0 1.0 multiply_convert_fusion.3
  43.0 0.3 reduce-scatter.5.cloned.1.call-start
  43.3 0.2 reduce-window.4
  43.5 0.1 dynamic-slice_bitcast_fusion
  43.6 0.7 gather_fusion
  44.3 0.1 convert_reduce_fusion
  44.4 0.1 select_reduce_fusion
  44.5 0.5 multiply_cosine_fusion
  45.0 2.0 broadcast_compare_fusion
  47.1 115.4 %all-gather.8.cloned.1.call-done = bf16[2,1024,1,3136]{3,1,0,2:T(8,128)(2,1)} async-done(((bf16[2,128,1,3136]{3,1,0,2:T(8,128)(2,1)}), bf16[2,1024,1,3136]{3,1,0,2:T(8,128)(2,1)}) %all-gather.8.cloned.1.call-update) | async-done | bytes 12845072 | tf_op jit(solution)/shard_map/all_gather | solution.py:79
  162.5 10.9 %copy.40 = bf16[32,2,32,3136]{3,2,1,0:T(8,128)(2,1)} copy(bf16[32,2,32,3136]{3,2,0,1:T(8,128)(2,1)} %bitcast.57) | data formatting | bytes 25690112 | tf_op jit(solution)/shard_map/reshape | solution.py:81
  173.4 5.5 broadcast_in_dim.117
  178.9 38.4 %scatter_fusion = bf16[2,32,32,3136]{3,2,1,0:T(8,128)(2,1)} fusion(bf16[2,32,32,3136]{3,2,1,0:T(8,128)(2,1)} %broadcast_in_dim.117, s32[32]{0:T(128)S(1)} %fusion.44, bf16[32,2,32,3136]{3,2,1,0:T(8,128)(2,1)} %copy.40), kind=kCustom, calls=%fused_computation.1 | custom fusion | bytes 38535296 | tf_op jit(solution)/shard_map/scatter | solution.py:82
  217.3 9.5 %fusion.72 = (bf16[1,32,32,3136]{3,2,1,0:T(8,128)(2,1)}, bf16[1,32,32,3136]{3,2,1,0:T(8,128)(2,1)}) fusion(bf16[2,32,32,3136]{3,2,1,0:T(8,128)(2,1)} %scatter_fusion), kind=kLoop, calls=%fused_computation.121 | loop fusion | bytes 25690112 | tf_op jit(solution)/shard_map/slice | solution.py:100
  226.8 3.9 fusion.32
  230.7 0.1 fusion.74
  230.9 0.1 slice.272
  231.0 1.1 subtract_convert_fusion.3
  232.1 9.7 %fusion.78 = f32[4,1024]{1,0:T(4,128)S(1)} fusion(f32[4]{0:T(128)S(1)} %get-tuple-element.43, f32[4]{0:T(128)S(1)} %get-tuple-element.42, pred[1024,1024]{0,1:T(8,128)(4,1)S(1)} %get-tuple-element.44, pred[1024,1024]{0,1:T(8,128)(4,1)} %get-tuple-element.45, bf16[1024,4,32]{0,2,1:T(8,128)(2,1)} %get-tuple-element.30, ...), kind=kOutput, calls=%fused_computation.127 | convolution fusion | flops 564134912 | bytes 3162144 | tf_op jit(solution)/shard_map/sub | solution.py:128
  241.8 10.5 %fusion.37 = bf16[4,64,1024]{2,1,0:T(8,128)(2,1)S(1)} fusion(bf16[1024,4,64]{0,2,1:T(8,128)(2,1)S(1)} %bitcast.73, f32[4,1024]{1,0:T(4,128)S(1)} %fusion.78, f32[4]{0:T(128)S(1)} %get-tuple-element.43, f32[4]{0:T(128)S(1)} %get-tuple-element.42, pred[1024,1024]{0,1:T(8,128)(4,1)S(1)} %get-tuple-element.44, pred[1024,1024]{0,1:T(8,128)(4,1)} %get-tuple-element.45, ...), kind=kOutput, calls=%fused_computation.49 | convolution fusion | flops 1105466368 | bytes 4210720 | tf_op jit(solution)/shard_map/hqk,khd->qhd/dot_general | solution.py:133
  252.3 3.2 convolution_convert_fusion.1
  255.6 33.6 %reduce-scatter.5.cloned.1.call-done = bf16[256,1024]{1,0:T(8,128)(2,1)} async-done(((bf16[1024,1024]{1,0:T(8,128)(2,1)}), bf16[256,1024]{1,0:T(8,128)(2,1)}) %reduce-scatter.5.cloned.1.call-update) | async-done | bytes 524304 | tf_op jit(solution)/shard_map/reduce_scatter | solution.py:137
  289.1 1.3 multiply_reduce_fusion.2
  290.4 2.0 multiply_convert_fusion.2
  292.5 0.5 reduce-scatter.7.cloned.1.call-start
  293.0 35.0 %all-gather.10.cloned.1.call-done = bf16[1024,1024]{1,0:T(8,128)(2,1)} async-done(((bf16[256,1024]{1,0:T(8,128)(2,1)}), bf16[1024,1024]{1,0:T(8,128)(2,1)}) %all-gather.10.cloned.1.call-update) | async-done | bytes 2097168 | tf_op jit(solution)/shard_map/all_gather | solution.py:146
  327.9 5.8 %fusion.22 = f32[1024,1408]{1,0:T(8,128)S(1)} fusion(bf16[1024,1024]{1,0:T(8,128)(2,1)} %all-gather.10.cloned.1.call-done, bf16[1024,3136]{1,0:T(8,128)(2,1)} %bitcast.64), kind=kOutput, calls=%fused_computation.32 | convolution fusion | flops 2952790016 | bytes 10747904 | tf_op jit(solution)/shard_map/dot_general | solution.py:44
  333.8 4.7 convolution_convert_fusion.3
  338.6 35.3 %reduce-scatter.7.cloned.1.call-done = bf16[256,1024]{1,0:T(8,128)(2,1)} async-done(((bf16[1024,1024]{1,0:T(8,128)(2,1)}), bf16[256,1024]{1,0:T(8,128)(2,1)}) %reduce-scatter.7.cloned.1.call-update) | async-done | bytes 524304 | tf_op jit(solution)/shard_map/reduce_scatter | solution.py:148
  373.9 1.3 multiply_reduce_fusion.1
  375.2 1.0 multiply_convert_fusion.1
  376.3 35.4 %all-gather.12.cloned.1.call-done = bf16[1024,1024]{1,0:T(8,128)(2,1)} async-done(((bf16[256,1024]{1,0:T(8,128)(2,1)}), bf16[1024,1024]{1,0:T(8,128)(2,1)}) %all-gather.12.cloned.1.call-update) | async-done | bytes 2097168 | tf_op jit(solution)/shard_map/all_gather | solution.py:107
  411.7 3.9 fusion.29
  415.6 0.1 fusion.73
  415.7 0.1 slice.271
  415.8 1.1 subtract_convert_fusion.1
  416.9 9.7 %fusion.79 = f32[4,1024]{1,0:T(4,128)S(1)} fusion(f32[4]{0:T(128)S(1)} %get-tuple-element.41, f32[4]{0:T(128)S(1)} %get-tuple-element.40, pred[1024,1024]{0,1:T(8,128)(4,1)} %copy-done.5, pred[1024,1024]{0,1:T(8,128)(4,1)} %get-tuple-element.45, bf16[1024,4,32]{0,2,1:T(8,128)(2,1)} %get-tuple-element.28, bf16[1024,4,32]{0,2,1:T(8,128)(2,1)} %get-tuple-element.29, ...), kind=kOutput, calls=%fused_computation.128 | convolution fusion | flops 564134912 | bytes 3162144 | tf_op jit(solution)/shard_map/sub | solution.py:128
  426.6 10.5 %fusion.36 = bf16[4,64,1024]{2,1,0:T(8,128)(2,1)S(1)} fusion(bf16[1024,4,64]{0,2,1:T(8,128)(2,1)S(1)} %bitcast.72, f32[4,1024]{1,0:T(4,128)S(1)} %fusion.79, f32[4]{0:T(128)S(1)} %get-tuple-element.41, f32[4]{0:T(128)S(1)} %get-tuple-element.40, pred[1024,1024]{0,1:T(8,128)(4,1)} %copy-done.5, pred[1024,1024]{0,1:T(8,128)(4,1)} %get-tuple-element.45, ...), kind=kOutput, calls=%fused_computation.48 | convolution fusion | flops 1105466368 | bytes 4210720 | tf_op jit(solution)/shard_map/hqk,khd->qhd/dot_general | solution.py:133
  437.1 3.1 convolution_convert_fusion
  440.3 35.3 %reduce-scatter.9.cloned.1.call-done = bf16[256,1024]{1,0:T(8,128)(2,1)} async-done(((bf16[1024,1024]{1,0:T(8,128)(2,1)}), bf16[256,1024]{1,0:T(8,128)(2,1)}) %reduce-scatter.9.cloned.1.call-update) | async-done | bytes 524304 | tf_op jit(solution)/shard_map/reduce_scatter | solution.py:137
  475.6 1.3 multiply_reduce_fusion
  476.9 2.0 multiply_convert_fusion
  479.0 0.3 reduce-scatter.11.cloned.1.call-start
  479.2 35.2 %all-gather.14.cloned.1.call-done = bf16[1024,1024]{1,0:T(8,128)(2,1)} async-done(((bf16[256,1024]{1,0:T(8,128)(2,1)}), bf16[1024,1024]{1,0:T(8,128)(2,1)}) %all-gather.14.cloned.1.call-update) | async-done | bytes 2097168 | tf_op jit(solution)/shard_map/all_gather | solution.py:146
  514.4 5.9 %fusion.20 = f32[1024,1408]{1,0:T(8,128)S(1)} fusion(bf16[1024,1024]{1,0:T(8,128)(2,1)} %all-gather.14.cloned.1.call-done, bf16[1024,3136]{1,0:T(8,128)(2,1)} %bitcast.60), kind=kOutput, calls=%fused_computation.30 | convolution fusion | flops 2952790016 | bytes 10747904 | tf_op jit(solution)/shard_map/dot_general | solution.py:44
  520.3 4.7 convolution_convert_fusion.2
  525.0 35.4 %reduce-scatter.11.cloned.1.call-done = bf16[256,1024]{1,0:T(8,128)(2,1)} async-done(((bf16[1024,1024]{1,0:T(8,128)(2,1)}), bf16[256,1024]{1,0:T(8,128)(2,1)}) %reduce-scatter.11.cloned.1.call-update) | async-done | bytes 524304 | tf_op jit(solution)/shard_map/reduce_scatter | solution.py:148
  560.4 2.2 convert_add_fusion
  (56 shorter events, 0.5 us)
Async XLA Ops:
  6.5 37.0 %copy-start = (s32[32]{0:T(128)S(1)}, s32[32]{0:T(128)}, u32[]{:S(2)}) copy-start(s32[32]{0:T(128)} %param.8) | copy-start | bytes 388
  6.5 155.9 %all-gather.8.cloned.1.call-start = ((), (), s32[]{:S(2)}) async-start(), calls=%async_computation.6 | async-start | bytes 14745600 | tf_op jit(solution)/shard_map/all_gather | solution.py:79
  14.5 27.3 %copy-start.2 = (f32[256,1024]{1,0:T(8,128)S(1)}, f32[256,1024]{1,0:T(8,128)}, u32[]{:S(2)}) copy-start(f32[256,1024]{1,0:T(8,128)} %param.9) | copy-start | bytes 3145732
  14.5 27.5 %copy-start.11 = (f32[2,2,1024]{2,1,0:T(2,128)S(1)}, f32[2,2,1024]{2,1,0:T(2,128)}, u32[]{:S(2)}) copy-start(f32[2,2,1024]{2,1,0:T(2,128)} %param.10) | copy-start | bytes 49156
  14.7 28.6 %copy-start.13 = (s32[1,4]{1,0:T(1,128)S(1)}, s32[1,4]{1,0:T(1,128)}, u32[]{:S(2)}) copy-start(s32[1,4]{1,0:T(1,128)} %param.11) | copy-start | bytes 52
  14.7 28.8 %copy-start.12 = (f32[2,16,2]{1,2,0:T(2,128)S(1)}, f32[2,16,2]{1,2,0:T(2,128)}, u32[]{:S(2)}) copy-start(f32[2,16,2]{1,2,0:T(2,128)} %param.13) | copy-start | bytes 772
  14.7 30.3 %copy-start.10 = (s32[1024]{0:T(1024)S(1)}, s32[1024]{0:T(1024)}, u32[]{:S(2)}) copy-start(s32[1024]{0:T(1024)} %param.12) | copy-start | bytes 12292
  41.7 185.1 %all-gather.6.cloned.1.call-start = ((), (), s32[]{:S(2)}) async-start(), calls=%async_computation.5 | async-start | bytes 2621440 | tf_op jit(solution)/shard_map/all_gather | solution.py:107
  43.0 246.1 %reduce-scatter.5.cloned.1.call-start = ((), (), s32[]{:S(2)}) async-start(), calls=%async_computation.7 | async-start | bytes 2621440 | tf_op jit(solution)/shard_map/reduce_scatter | solution.py:137
  47.1 194.7 %copy-start.5 = (pred[1024,1024]{0,1:T(8,128)(4,1)}, pred[1024,1024]{0,1:T(8,128)(4,1)S(1)}, u32[]{:S(2)}) copy-start(pred[1024,1024]{0,1:T(8,128)(4,1)S(1)} %get-tuple-element.44) | copy-start | bytes 3145732
  232.1 9.7 %copy-start.8 = (bf16[1024,4,32]{0,2,1:T(8,128)(2,1)}, bf16[1024,4,32]{0,2,1:T(8,128)(2,1)S(1)}, u32[]{:S(2)}) copy-start(bf16[1024,4,32]{0,2,1:T(8,128)(2,1)S(1)} %get-tuple-element.24) | copy-start | bytes 786436
  232.1 9.7 %copy-start.9 = (bf16[1024,4,32]{0,2,1:T(8,128)(2,1)}, bf16[1024,4,32]{0,2,1:T(8,128)(2,1)S(1)}, u32[]{:S(2)}) copy-start(bf16[1024,4,32]{0,2,1:T(8,128)(2,1)S(1)} %get-tuple-element.25) | copy-start | bytes 786436
  255.5 72.4 %all-gather.10.cloned.1.call-start = ((), (), s32[]{:S(2)}) async-start(), calls=%async_computation.8 | async-start | bytes 2621440 | tf_op jit(solution)/shard_map/all_gather | solution.py:146
  292.5 81.4 %reduce-scatter.7.cloned.1.call-start = ((), (), s32[]{:S(2)}) async-start(), calls=%async_computation.9 | async-start | bytes 2621440 | tf_op jit(solution)/shard_map/reduce_scatter | solution.py:148
  333.8 40.1 %copy-start.3 = (bf16[256,1024]{1,0:T(8,128)(2,1)S(1)}, bf16[256,1024]{1,0:T(8,128)(2,1)}, u32[]{:S(2)}) copy-start(bf16[256,1024]{1,0:T(8,128)(2,1)} %reduce-scatter.5.cloned.1.call-done) | copy-start | bytes 1572868
  338.5 73.2 %all-gather.12.cloned.1.call-start = ((), (), s32[]{:S(2)}) async-start(), calls=%async_computation.10 | async-start | bytes 2621440 | tf_op jit(solution)/shard_map/all_gather | solution.py:107
  376.2 99.4 %reduce-scatter.9.cloned.1.call-start = ((), (), s32[]{:S(2)}) async-start(), calls=%async_computation.11 | async-start | bytes 2621440 | tf_op jit(solution)/shard_map/reduce_scatter | solution.py:137
  416.9 9.7 %copy-start.6 = (bf16[1024,4,32]{0,2,1:T(8,128)(2,1)S(1)}, bf16[1024,4,32]{0,2,1:T(8,128)(2,1)}, u32[]{:S(2)}) copy-start(bf16[1024,4,32]{0,2,1:T(8,128)(2,1)} %get-tuple-element.28) | copy-start | bytes 786436
  416.9 9.7 %copy-start.7 = (bf16[1024,4,32]{0,2,1:T(8,128)(2,1)S(1)}, bf16[1024,4,32]{0,2,1:T(8,128)(2,1)}, u32[]{:S(2)}) copy-start(bf16[1024,4,32]{0,2,1:T(8,128)(2,1)} %get-tuple-element.29) | copy-start | bytes 786436
  440.3 74.2 %all-gather.14.cloned.1.call-start = ((), (), s32[]{:S(2)}) async-start(), calls=%async_computation.12 | async-start | bytes 2621440 | tf_op jit(solution)/shard_map/all_gather | solution.py:146
  479.0 81.4 %reduce-scatter.11.cloned.1.call-start = ((), (), s32[]{:S(2)}) async-start(), calls=%async_computation.13 | async-start | bytes 2621440 | tf_op jit(solution)/shard_map/reduce_scatter | solution.py:148
  520.3 40.1 %copy-start.4 = (bf16[256,1024]{1,0:T(8,128)(2,1)S(1)}, bf16[256,1024]{1,0:T(8,128)(2,1)}, u32[]{:S(2)}) copy-start(bf16[256,1024]{1,0:T(8,128)(2,1)} %reduce-scatter.9.cloned.1.call-done) | copy-start | bytes 1572868
  520.3 42.3 %copy-start.1 = (s32[32]{0:T(128)S(1)}, s32[32]{0:T(128)}, u32[]{:S(2)}) copy-start(s32[32]{0:T(128)} %param.8) | copy-start | bytes 388
Sparse Core Ops, SparseCore 0:
  41.9 120.5 all-gather.7
  164.3 33.4 all-gather.5
  255.6 33.4 reduce-scatter.4
  292.6 35.3 all-gather.9
  338.6 35.1 reduce-scatter.6
  376.3 35.2 all-gather.11
  440.4 35.1 reduce-scatter.8
  479.1 35.2 all-gather.13
  525.1 35.1 reduce-scatter.10
where the time goes:
time: 574 us; the launch traced here: 569 us
  waiting for transfers between devices  361 us (63%)
  matrix products  75.5 us (13%)
  local copies, waits for them, and re-layouts  72.9 us (13%)
  blocking collectives  25.7 us (4%)
  other arithmetic  19.6 us (3%)
  between operations  13.8 us (2%)
    all_gather x1, waiting for transfers between devices, on_device(): collected = lax.all_gather(regrouped, 'seq', axis=1, tiled=True)  115 us
    reduce_scatter x2, waiting for transfers between devices, on_device(): lax.psum_scatter(project_out(source=hidden, weight=down_weight).astype(jn...  70.7 us
    all_gather x2, waiting for transfers between devices, on_device(): lax.all_gather(normed_mlp, 'tp', axis=0, tiled=True)  70.2 us
    reduce_scatter x2, waiting for transfers between devices, on_device(): lax.psum_scatter(project_out(source=mixed_heads, weight=out_weight).astyp...  68.9 us
    scatter x1, local copies, waits for them, and re-layouts, on_device(): placed = jnp.zeros_like(blocks).at[:, shard_order[slot_index]].set(blocks)  38.4 us
    all_gather x2, waiting for transfers between devices, on_device(): lax.all_gather(normed, 'tp', axis=0, tiled=True)  35.4 us
    all_to_all x1, blocking collectives, on_device(): lax.all_to_all(grouped, 'tp', split_axis=2, concat_axis=1, tiled=True)  25.7 us
    dot_general x2, matrix products, on_device(): jnp.einsum('hqk,khd->qhd', attn_weights, values, preferred_element_type=j...  21 us
  transfers between devices with their start and end apart: 9, of which 8 were waited for; matrix products, arithmetic and copies ran while one was open for 12% of the time, Pallas kernels for 0%

commit v1 on v0

--- a/solution.py
+++ b/solution.py
@@ -1,6 +1,10 @@
+import functools
+
 import jax
 import jax.numpy as jnp
 from jax import lax
+from jax.experimental import pallas as pl
+from jax.experimental.pallas import tpu as pltpu
 from jax.sharding import PartitionSpec as P
 
 NEGATIVE = -1e30
@@ -27,7 +31,10 @@
 
 
 def prompt_layout(lengths, token_count):
-    prompt_ends = jnp.cumsum(lengths)
+    order = jnp.arange(lengths.shape[0])
+    prompt_ends = jnp.sum(
+        jnp.where(order[:, None] >= order[None, :], lengths[None, :], 0), axis=1
+    )
     prompt_starts = prompt_ends - lengths
     positions = jnp.arange(token_count, dtype=jnp.int32)
     segment = jnp.sum((positions[:, None] >= prompt_ends[None, :]).astype(jnp.int32), axis=1)
@@ -49,6 +56,120 @@
 def project_out(source, weight):
     return lax.dot_general(
         source, weight, (((1,), (1,)), ((), ())), preferred_element_type=jnp.float32
+    )
+
+
+CHUNKS = 2
+MESH = pl.DeviceIdType.MESH
+
+
+def exchange_kernel(n, reduce, gather, *refs):
+    refs = list(refs)
+    part = refs.pop(0) if reduce else None
+    residual = refs.pop(0)
+    gain = refs.pop(0) if gather else None
+    new_residual = refs.pop(0) if reduce else None
+    gathered = refs.pop(0) if gather else None
+    if reduce:
+        slots, part_sent, part_got = refs[:3]
+        refs = refs[3:]
+    if gather:
+        held, norm_sent, norm_got = refs
+    rows = residual.shape[0]
+    step = rows // CHUNKS
+    me = lax.axis_index("tp")
+    seq = lax.axis_index("seq")
+    peers = [lax.rem(me + k, n) for k in range(1, n)]
+
+    barrier = pltpu.get_barrier_semaphore()
+    for peer in peers:
+        pl.semaphore_signal(barrier, inc=1, device_id=(seq, peer), device_id_type=MESH)
+    pl.semaphore_wait(barrier, n - 1)
+
+    part_copies, norm_copies = [], []
+    if reduce:
+        for c in range(CHUNKS):
+            for k in range(n - 1):
+                start = pl.multiple_of(peers[k] * rows + c * step, step)
+                copy = pltpu.make_async_remote_copy(
+                    src_ref=part.at[pl.ds(start, step)],
+                    dst_ref=slots.at[c, k],
+                    send_sem=part_sent.at[c, k],
+                    recv_sem=part_got.at[c, k],
+                    device_id=(seq, peers[k]),
+                    device_id_type=MESH,
+                )
+                copy.start()
+                part_copies.append(copy)
+    for c in range(CHUNKS):
+        mine = pl.ds(pl.multiple_of(me * rows + c * step, step), step)
+        values = residual[pl.ds(c * step, step)]
+        if reduce:
+            total = part[mine].astype(jnp.float32)
+            for k in range(n - 1):
+                part_copies[c * (n - 1) + k].wait_recv()
+                total = total + slots[c, k].astype(jnp.float32)
+            values = values + total
+            new_residual[pl.ds(c * step, step)] = values
+        if gather:
+            held[mine] = rms_scaled(values, gain[...]).astype(jnp.bfloat16)
+            for k in range(n - 1):
+                copy = pltpu.make_async_remote_copy(
+                    src_ref=held.at[mine],
+                    dst_ref=held.at[mine],
+                    send_sem=norm_sent.at[c, k],
+                    recv_sem=norm_got.at[c, k],
+                    device_id=(seq, peers[k]),
+                    device_id_type=MESH,
+                )
+                copy.start()
+                norm_copies.append(copy)
+    for copy in norm_copies:
+        copy.wait_recv()
+    if gather:
+        gathered[...] = held[...]
+    for copy in part_copies + norm_copies:
+        copy.wait_send()
+
+
+def exchange(n, residual, part=None, gain=None):
+    reduce, gather = part is not None, gain is not None
+    rows, width = residual.shape
+    args = [residual]
+    outs, scratch = [], []
+    copies = pltpu.SemaphoreType.DMA((CHUNKS, n - 1))
+    if reduce:
+        args = [part] + args
+        outs.append(jax.ShapeDtypeStruct((rows, width), jnp.float32))
+        scratch += [pltpu.VMEM((CHUNKS, n - 1, rows // CHUNKS, width), jnp.bfloat16), copies, copies]
+    if gather:
+        args.append(gain)
+        outs.append(jax.ShapeDtypeStruct((n * rows, width), jnp.bfloat16))
+        scratch += [pltpu.VMEM((n * rows, width), jnp.bfloat16), copies, copies]
+    vmem = pl.BlockSpec(memory_space=pltpu.VMEM)
+    sides = int(reduce) + int(gather)
+    return pl.pallas_call(
+        functools.partial(exchange_kernel, n, reduce, gather),
+        out_shape=outs,
+        in_specs=[vmem] * len(args),
+        out_specs=[vmem] * len(outs),
+        scratch_shapes=scratch,
+        compiler_params=pltpu.CompilerParams(
+            collective_id=int(reduce) + 2 * int(gather),
+            has_side_effects=True,
+            vmem_limit_bytes=24 * 1024 * 1024,
+        ),
+        cost_estimate=pl.CostEstimate(
+            flops=10 * rows * width,
+            bytes_accessed=sides * 64 * 1024 * 1024,
+            transcendentals=0,
+        ),
+    )(*args)
+
+
+def permuted(values, matrix):
+    return jnp.dot(
+        values, matrix, precision=lax.Precision.HIGHEST, preferred_element_type=jnp.float32
     )
 
 
@@ -62,25 +183,49 @@
     ff_width = (total_cols - 4 * model_width) // 3
     head_cols = model_width // tp_count
     unit_cols = ff_width // tp_count
-    rounded = trainer_rows.astype(jnp.bfloat16)
-    part_widths = [model_width] * 4 + [ff_width] * 3
-    grouped_parts = []
-    column_start = 0
-    for part_width in part_widths:
-        grouped_parts.append(
-            rounded[:, :, column_start : column_start + part_width].reshape(
-                layer_count, block_rows, tp_count, part_width // tp_count
+    widths = [model_width] * 4 + [ff_width] * 3
+    starts = [sum(widths[:i]) for i in range(len(widths))]
+
+    def by_owner(layer, parts):
+        pieces = []
+        for i in parts:
+            piece = trainer_rows[layer, :, starts[i] : starts[i] + widths[i]].astype(jnp.bfloat16)
+            pieces.append(
+                piece.reshape(block_rows, tp_count, widths[i] // tp_count).transpose(1, 0, 2)
             )
-        )
-        column_start = column_start + part_width
-    grouped = jnp.concatenate(grouped_parts, axis=3)
-    slot_index = jnp.arange(seq_count * tp_count, dtype=jnp.int32)
-    regrouped = lax.all_to_all(grouped, "tp", split_axis=2, concat_axis=1, tiled=True)
-    collected = lax.all_gather(regrouped, "seq", axis=1, tiled=True)
-    local_cols = collected.shape[3]
-    blocks = collected.reshape(layer_count, seq_count * tp_count, block_rows, local_cols)
-    placed = jnp.zeros_like(blocks).at[:, shard_order[slot_index]].set(blocks)
-    weights = placed.reshape(layer_count, model_width, local_cols)
+        return pieces
+
+    def swap(pieces):
+        swapped = lax.all_to_all(
+            jnp.concatenate(pieces, axis=2), "tp", split_axis=0, concat_axis=1, tiled=True
+        )
+        return swapped[0]
+
+    def over_seq(piece):
+        return lax.all_gather(piece, "seq", axis=0, tiled=True)
+
+    first = over_seq(swap(by_owner(0, range(4))))
+    later = by_owner(0, range(4, 7))
+    for layer in range(1, layer_count):
+        later = later + by_owner(layer, range(7))
+    later = swap(later)
+    attention_weights, mlp_weights = [first], []
+    at = 0
+    for layer in range(layer_count):
+        if layer > 0:
+            attention_weights.append(over_seq(later[:, at : at + 4 * head_cols]))
+            at = at + 4 * head_cols
+        mlp_weights.append(over_seq(later[:, at : at + 3 * unit_cols]))
+        at = at + 3 * unit_cols
+
+    column = jnp.arange(model_width, dtype=jnp.int32)
+    rows_in_block = model_width // shard_order.shape[0]
+    row_of = (
+        shard_order[:, None] * rows_in_block
+        + jnp.arange(rows_in_block, dtype=jnp.int32)[None, :]
+    ).reshape(model_width)
+    to_trainer = (column[:, None] == row_of[None, :]).astype(jnp.float32)
+    gains = permuted(norm_gains.reshape(2 * layer_count, model_width), to_trainer)
     token_count = variate_ids.shape[0]
     segment, offsets = prompt_layout(prompt_lengths[0], token_count)
     same_prompt = segment[:, None] == segment[None, :]
@@ -91,21 +236,20 @@
     bias_table = lax.dynamic_slice_in_dim(
         variate_bias, lax.axis_index("tp") * local_heads, local_heads, 1
     )
-    residual = residual_in
+    residual = permuted(residual_in, to_trainer)
+    [gathered] = exchange(tp_count, residual, gain=gains[:1])
     for layer_index in range(layer_count):
         layer_bias = bias_table[layer_index]
         pair_bias = jnp.where(
             same_variate[None], layer_bias[:, 1][:, None, None], layer_bias[:, 0][:, None, None]
         )
-        layer_weights = weights[layer_index]
+        layer_weights = attention_weights[layer_index]
         qkv_weight = layer_weights[:, : 3 * head_cols]
-        out_weight = layer_weights[:, 3 * head_cols : 4 * head_cols]
-        gate_up_weight = layer_weights[:, 4 * head_cols : 4 * head_cols + 2 * unit_cols]
-        down_weight = layer_weights[:, 4 * head_cols + 2 * unit_cols :]
-        normed = rms_scaled(residual, norm_gains[layer_index, 0]).astype(jnp.bfloat16)
-        projected = project_rows(
-            lax.all_gather(normed, "tp", axis=0, tiled=True), weight=qkv_weight
-        )
+        out_weight = layer_weights[:, 3 * head_cols :]
+        layer_weights = mlp_weights[layer_index]
+        gate_up_weight = layer_weights[:, : 2 * unit_cols]
+        down_weight = layer_weights[:, 2 * unit_cols :]
+        projected = project_rows(gathered, weight=qkv_weight)
         queries = rotate(
             projected[:, :head_cols].reshape(token_count, local_heads, head_size), offsets
         ).astype(jnp.bfloat16)
@@ -134,25 +278,19 @@
             .astype(jnp.bfloat16)
             .reshape(token_count, head_cols)
         )
-        head_total = lax.psum_scatter(
-            project_out(source=mixed_heads, weight=out_weight).astype(jnp.bfloat16),
-            "tp",
-            scatter_dimension=0,
-            tiled=True,
-        ).astype(jnp.float32)
-        residual = residual + head_total
-        normed_mlp = rms_scaled(residual, norm_gains[layer_index, 1]).astype(jnp.bfloat16)
-        hidden = gated_units(
-            lax.all_gather(normed_mlp, "tp", axis=0, tiled=True), weight=gate_up_weight
-        )
-        unit_total = lax.psum_scatter(
-            project_out(source=hidden, weight=down_weight).astype(jnp.bfloat16),
-            "tp",
-            scatter_dimension=0,
-            tiled=True,
-        ).astype(jnp.float32)
-        residual = residual + unit_total
-    return residual
+        head_part = project_out(source=mixed_heads, weight=out_weight).astype(jnp.bfloat16)
+        residual, gathered = exchange(
+            tp_count, residual, head_part, gains[2 * layer_index + 1 : 2 * layer_index + 2]
+        )
+        hidden = gated_units(gathered, weight=gate_up_weight)
+        unit_part = project_out(source=hidden, weight=down_weight).astype(jnp.bfloat16)
+        if layer_index + 1 < layer_count:
+            residual, gathered = exchange(
+                tp_count, residual, unit_part, gains[2 * layer_index + 2 : 2 * layer_index + 3]
+            )
+        else:
+            [residual] = exchange(tp_count, residual, unit_part)
+    return permuted(residual, to_trainer.T)
 
 
 def solution(mesh):

time: 574 us -> 346 us (0.60)
  waiting for transfers between devices: 361 us -> 0.07 us
  Pallas kernels: 0 us -> 189 us
  local copies, waits for them, and re-layouts: 72.9 us -> 22.4 us
  other arithmetic: 19.6 us -> 7.85 us
    all_gather x5 -> x4, waiting for transfers between devices: 221 us -> 0.01 us  [over_seq(): return lax.all_gather(piece, 'seq', axis=0, tiled=True)]
    pallas_call x0 -> x5, Pallas kernels: none -> 189 us  [exchange(): pl.pallas_call(functools.partial(exchange_kernel, n, reduce, gather), out...]
    reduce_scatter x4 -> x0, waiting for transfers between devices: 140 us -> none  [the longest x2 70.7 us: on_device(): lax.psum_scatter(project_out(source=hidden, weight=down_weight).astype(jn...]
    scatter x1 -> x0, local copies, waits for them, and re-layouts: 38.4 us -> none  [on_device(): placed = jnp.zeros_like(blocks).at[:, shard_order[slot_index]].set(blocks)]
    reshape x8 -> x1, local copies, waits for them, and re-layouts: 12.6 us -> 0.02 us  [on_device(): norm_gains.reshape(2 * layer_count, model_width)]
    convert_element_type x5 -> x0, other arithmetic: 8.09 us -> none  [the longest x2 4.07 us: on_device(): rms_scaled(residual, norm_gains[layer_index, 1]).astype(jnp.bfloat16)]
    slice x4 -> x5, local copies, waits for them, and re-layouts: 9.7 us -> 2.95 us  [the longest x1 1.2 us: on_device(): mlp_weights.append(over_seq(later[:, at:at + 3 * unit_cols]))]
    convert_element_type x0 -> x14, local copies, waits for them, and re-layouts: none -> 6.75 us  [by_owner(): trainer_rows[layer, :, starts[i]:starts[i] + widths[i]].astype(jnp.bfloat16)]
  transfers between devices with their start and end apart: 9 -> 4, of which waited for: 8 -> 0; matrix products, arithmetic and copies ran while one was open for 12% -> 26% of each run, Pallas kernels for 0% -> 48%
where the time goes in v1:
time: 346 us; the launch traced here: 342 us
  Pallas kernels  189 us (55%)
  matrix products  78.4 us (23%)
  blocking collectives  29.7 us (9%)
  local copies, waits for them, and re-layouts  22.4 us (6%)
  between operations  13.8 us (4%)
  other arithmetic  7.85 us (2%)
    pallas_call x5, Pallas kernels, exchange(): pl.pallas_call(functools.partial(exchange_kernel, n, reduce, gather), out...  189 us
    all_to_all x2, blocking collectives, swap(): lax.all_to_all(jnp.concatenate(pieces, axis=2), 'tp', split_axis=0, conca...  29.7 us
    dot_general x2, matrix products, on_device(): jnp.einsum('hqk,khd->qhd', attn_weights, values, preferred_element_type=j...  21.4 us
    sub x2, matrix products, on_device(): weights_exp = jnp.exp(scores - row_peak)  19.3 us
    dot_general x2, matrix products, gated_units(): gate_up = jnp.dot(row_piece, weight, preferred_element_type=jnp.float32)  12.2 us
    dot_general x4, matrix products, project_out(): lax.dot_general(source, weight, (((1,), (1,)), ((), ())), preferred_eleme...  10.5 us
    dot_general x2, matrix products, project_rows(): return jnp.dot(row_piece, weight, preferred_element_type=jnp.float32)  8.26 us
  transfers between devices with their start and end apart: 4, of which 0 were waited for; matrix products, arithmetic and copies ran while one was open for 26% of the time, Pallas kernels for 48%

profile of v1, /device:TPU:0, one launch (start us, length us, event | category | flops | bytes accessed | tf_op | source)
XLA Modules:
  0.0 342.1 jit_solution(8300227995014039301)
XLA Ops:
  6.5 2.2 convert.46
  8.7 0.1 fusion.81
  8.9 0.1 pad_maximum_fusion.4
  9.1 0.1 copy.25
  9.1 10.8 %all_to_all.8 = bf16[4,32,1024]{2,1,0:T(8,128)(2,1)} all-to-all(bf16[4,32,1024]{2,1,0:T(8,128)(2,1)S(1)} %copy.25), channel_id=1, replica_groups=mesh['seq'=8,'tp'=4] {'tp'}, dimensions={0} | all-to-all | bytes 524288 | tf_op jit(solution)/shard_map/all_to_all | solution.py:199
  19.9 0.0 all-gather.5.cloned.1.call-update
  20.0 0.0 all-gather.7.cloned.1.call-start
  20.0 0.7 convert_element_type.146
  20.7 0.6 convert_element_type.147
  21.3 0.7 convert_element_type.148
  22.0 0.7 convert_element_type.149
  22.6 0.8 fusion.82
  23.5 1.2 convert_element_type.143
  24.6 0.2 convert_element_type.144
  24.9 0.2 convert_element_type.145
  25.1 0.2 convert_element_type.150
  25.4 1.2 convert_element_type.151
  26.6 0.9 convert_element_type.152
  27.5 4.7 %concatenate.25 = bf16[4,32,5248]{2,0,1:T(4,128)(2,1)S(1)} concatenate(bf16[4,32,704]{2,0,1:T(4,128)(2,1)S(1)} %bitcast.69, bf16[4,32,704]{2,0,1:T(4,128)(2,1)S(1)} %bitcast.70, bf16[4,32,704]{2,0,1:T(4,128)(2,1)S(1)} %bitcast.71, bf16[4,32,256]{2,0,1:T(4,128)(2,1)} %bitcast.79, bf16[4,32,256]{2,0,1:T(4,128)(2,1)} %bitcast.80, bf16[4,32,256]{2,0,1:T(4,128)(2,1)} %bitcast.81, ...), dimensions={2} | concatenate | bytes 2686976 | tf_op jit(solution)/shard_map/concatenate | solution.py:200
  32.2 0.1 copy.27
  32.4 18.9 %all_to_all.9 = bf16[4,32,5248]{2,1,0:T(8,128)(2,1)S(1)} all-to-all(bf16[4,32,5248]{2,1,0:T(8,128)(2,1)S(1)} %copy.27), channel_id=1, replica_groups=mesh['seq'=8,'tp'=4] {'tp'}, dimensions={0} | all-to-all | bytes 2686976 | tf_op jit(solution)/shard_map/all_to_all | solution.py:199
  51.3 1.2 fusion.83
  52.6 0.0 all-gather.9.cloned.1.call-start
  52.6 0.8 slice.259
  53.5 0.6 all-gather.11.cloned.1.call-start
  54.1 0.1 iota_add_fusion
  54.1 0.1 add.51
  54.3 1.4 fusion.45
  55.7 2.1 fusion.42.refs_0_.refs_1_
  57.8 23.3 %shard_map.73 = bf16[1024,1024]{1,0:T(8,128)(2,1)S(1)} custom-call(f32[256,1024]{1,0:T(8,128)S(1)} %fusion.42.refs_0_.refs_1_, f32[1,1024]{1,0:T(1,128)S(1)} %get-tuple-element.52.refs_1_), custom_call_target="tpu_custom_call" | custom-call | flops 2621440 | bytes 67108864 | tf_op jit(solution)/shard_map/pallas_call | solution.py:151
  81.1 1.3 copy-done.2
  82.4 0.1 dynamic-slice_bitcast_fusion
  82.5 0.1 select_reduce_fusion.1
  82.6 0.1 convert_reduce_fusion
  82.7 0.1 select_reduce_fusion
  82.8 0.5 multiply_cosine_fusion
  83.4 0.0 all-gather.11.cloned.1.call-update
  83.4 2.0 broadcast_compare_fusion
  85.5 4.4 %fusion.38 = f32[1024,768]{0,1:T(8,128)S(1)} fusion(bf16[1024,1024]{1,0:T(8,128)(2,1)} %copy-done.2, bf16[1024,1024]{1,0:T(8,128)(2,1)} %all-gather.5.cloned.1.call-done), kind=kOutput, calls=%fused_computation.51 | convolution fusion | flops 1610612736 | bytes 6815744 | tf_op jit(solution)/shard_map/dot_general | solution.py:47
  89.8 0.9 slice.326
  90.7 0.1 fusion.80
  90.8 1.3 subtract_convert_fusion.3
  92.2 9.6 %fusion.85 = f32[4,1024]{1,0:T(4,128)S(1)} fusion(f32[4]{0:T(128)S(1)} %get-tuple-element.60, f32[4]{0:T(128)S(1)} %get-tuple-element.59, pred[1024,1024]{0,1:T(8,128)(4,1)S(1)} %get-tuple-element.61, pred[1024,1024]{0,1:T(8,128)(4,1)} %get-tuple-element.62, bf16[1024,4,32]{0,2,1:T(8,128)(2,1)} %get-tuple-element.47, ...), kind=kOutput, calls=%fused_computation.120 | convolution fusion | flops 564134912 | bytes 3162144 | tf_op jit(solution)/shard_map/sub | solution.py:272
  101.8 10.5 %fusion.44 = bf16[4,64,1024]{2,1,0:T(8,128)(2,1)S(1)} fusion(bf16[1024,4,64]{0,2,1:T(8,128)(2,1)S(1)} %bitcast.76, f32[4,1024]{1,0:T(4,128)S(1)} %fusion.85, f32[4]{0:T(128)S(1)} %get-tuple-element.60, f32[4]{0:T(128)S(1)} %get-tuple-element.59, pred[1024,1024]{0,1:T(8,128)(4,1)S(1)} %get-tuple-element.61, pred[1024,1024]{0,1:T(8,128)(4,1)} %get-tuple-element.62, ...), kind=kOutput, calls=%fused_computation.55 | convolution fusion | flops 1105466368 | bytes 4210720 | tf_op jit(solution)/shard_map/hqk,khd->qhd/dot_general | solution.py:277
  112.3 1.8 convolution_convert_fusion.1.refs_0_
  114.1 47.3 %shard_map.74 = (f32[256,1024]{1,0:T(8,128)S(1)}, bf16[1024,1024]{1,0:T(8,128)(2,1)S(1)}) custom-call(bf16[1024,1024]{1,0:T(8,128)(2,1)S(1)} %convolution_convert_fusion.1.refs_0_, f32[256,1024]{1,0:T(8,128)S(1)} %fusion.42.refs_0_.refs_1_, f32[1,1024]{1,0:T(1,128)S(1)} %get-tuple-element.51.refs_2_), custom_call_target="tpu_custom_call" | custom-call | flops 2621440 | bytes 134217728 | tf_op jit(solution)/shard_map/pallas_call | solution.py:151
  161.4 1.4 copy-done.3
  162.8 6.2 %fusion.25 = f32[1024,1408]{1,0:T(8,128)S(1)} fusion(bf16[1024,1024]{1,0:T(8,128)(2,1)} %copy-done.3, bf16[1024,2112]{1,0:T(8,128)(2,1)} %all-gather.7.cloned.1.call-done), kind=kOutput, calls=%fused_computation.34 | convolution fusion | flops 2952790016 | bytes 10747904 | tf_op jit(solution)/shard_map/dot_general | solution.py:51
  169.0 3.4 convolution_convert_fusion.3.refs_0_
  172.3 47.4 %shard_map.75 = (f32[256,1024]{1,0:T(8,128)S(1)}, bf16[1024,1024]{1,0:T(8,128)(2,1)S(1)}) custom-call(bf16[1024,1024]{1,0:T(8,128)(2,1)S(1)} %convolution_convert_fusion.3.refs_0_, f32[256,1024]{1,0:T(8,128)S(1)} %get-tuple-element.12.refs_1_, f32[1,1024]{1,0:T(1,128)S(1)} %get-tuple-element.50.refs_2_), custom_call_target="tpu_custom_call" | custom-call | flops 2621440 | bytes 134217728 | tf_op jit(solution)/shard_map/pallas_call | solution.py:151
  219.8 1.4 copy-done.4
  221.1 3.9 %fusion.35 = f32[1024,768]{0,1:T(8,128)S(1)} fusion(bf16[1024,1024]{1,0:T(8,128)(2,1)} %copy-done.4, bf16[1024,1024]{1,0:T(8,128)(2,1)} %all-gather.9.cloned.1.call-done), kind=kOutput, calls=%fused_computation.48 | convolution fusion | flops 1610612736 | bytes 6815744 | tf_op jit(solution)/shard_map/dot_general | solution.py:47
  225.1 0.9 slice.325
  225.9 0.1 fusion.79
  226.1 1.3 subtract_convert_fusion.1
  227.4 9.7 %fusion.86 = f32[4,1024]{1,0:T(4,128)S(1)} fusion(f32[4]{0:T(128)S(1)} %get-tuple-element.58, f32[4]{0:T(128)S(1)} %get-tuple-element.57, pred[1024,1024]{0,1:T(8,128)(4,1)S(1)} %copy-done.7, pred[1024,1024]{0,1:T(8,128)(4,1)S(1)} %copy-done.8, bf16[1024,4,32]{0,2,1:T(8,128)(2,1)} %get-tuple-element.45, bf16[1024,4,32]{0,2,1:T(8,128)(2,1)} %get-tuple-element.46, ...), kind=kOutput, calls=%fused_computation.121 | convolution fusion | flops 564134912 | bytes 3162144 | tf_op jit(solution)/shard_map/sub | solution.py:272
  237.1 11.0 %fusion.43 = bf16[4,64,1024]{2,1,0:T(8,128)(2,1)} fusion(bf16[1024,4,64]{0,2,1:T(8,128)(2,1)} %bitcast.75, f32[4,1024]{1,0:T(4,128)S(1)} %fusion.86, f32[4]{0:T(128)S(1)} %get-tuple-element.58, f32[4]{0:T(128)S(1)} %get-tuple-element.57, pred[1024,1024]{0,1:T(8,128)(4,1)S(1)} %copy-done.7, pred[1024,1024]{0,1:T(8,128)(4,1)S(1)} %copy-done.8, ...), kind=kOutput, calls=%fused_computation.54 | convolution fusion | flops 1105466368 | bytes 4210720 | tf_op jit(solution)/shard_map/hqk,khd->qhd/dot_general | solution.py:277
  248.1 2.0 convolution_convert_fusion.refs_0_
  250.0 47.0 %shard_map.76 = (f32[256,1024]{1,0:T(8,128)S(1)}, bf16[1024,1024]{1,0:T(8,128)(2,1)S(1)}) custom-call(bf16[1024,1024]{1,0:T(8,128)(2,1)S(1)} %convolution_convert_fusion.refs_0_, f32[256,1024]{1,0:T(8,128)S(1)} %get-tuple-element.14.refs_1_, f32[1,1024]{1,0:T(1,128)S(1)} %get-tuple-element.49.refs_2_), custom_call_target="tpu_custom_call" | custom-call | flops 2621440 | bytes 134217728 | tf_op jit(solution)/shard_map/pallas_call | solution.py:151
  297.1 1.4 copy-done.5
  298.4 6.0 %fusion.23 = f32[1024,1408]{1,0:T(8,128)S(1)} fusion(bf16[1024,1024]{1,0:T(8,128)(2,1)} %copy-done.5, bf16[1024,2112]{1,0:T(8,128)(2,1)} %all-gather.11.cloned.1.call-done), kind=kOutput, calls=%fused_computation.32 | convolution fusion | flops 2952790016 | bytes 10747904 | tf_op jit(solution)/shard_map/dot_general | solution.py:51
  304.5 3.4 convolution_convert_fusion.2.refs_0_
  307.9 24.3 %shard_map.77 = f32[256,1024]{1,0:T(8,128)S(1)} custom-call(bf16[1024,1024]{1,0:T(8,128)(2,1)S(1)} %convolution_convert_fusion.2.refs_0_, f32[256,1024]{1,0:T(8,128)S(1)} %get-tuple-element.16.refs_1_), custom_call_target="tpu_custom_call" | custom-call | flops 2621440 | bytes 67108864 | tf_op jit(solution)/shard_map/pallas_call | solution.py:151
  332.2 3.2 fusion.18
  (47 shorter events, 0.3 us)
Async XLA Ops:
  6.5 49.1 %copy-start = (f32[256,1024]{1,0:T(8,128)S(1)}, f32[256,1024]{1,0:T(8,128)}, u32[]{:S(2)}) copy-start(f32[256,1024]{1,0:T(8,128)} %param.9) | copy-start | bytes 3145732
  6.5 78.9 %all-gather.5.cloned.1.call-start = ((), (), s32[]{:S(2)}) async-start(), calls=%async_computation.2 | async-start | bytes 2359296 | tf_op jit(solution)/shard_map/all_gather | solution.py:205
  20.0 142.8 %all-gather.7.cloned.1.call-start = ((), (), s32[]{:S(2)}) async-start(), calls=%async_computation.3 | async-start | bytes 5013504 | tf_op jit(solution)/shard_map/all_gather | solution.py:205
  32.2 21.8 %copy-start.14 = (s32[32]{0:T(128)S(1)}, s32[32]{0:T(128)}, u32[]{:S(2)}) copy-start(s32[32]{0:T(128)} %param.8) | copy-start | bytes 388
  32.2 22.0 %copy-start.12 = (f32[2,2,1024]{2,1,0:T(2,128)S(1)}, f32[2,2,1024]{2,1,0:T(2,128)}, u32[]{:S(2)}) copy-start(f32[2,2,1024]{2,1,0:T(2,128)} %param.10) | copy-start | bytes 49156
  52.5 29.9 %copy-start.13 = (f32[2,16,2]{1,2,0:T(2,128)S(1)}, f32[2,16,2]{1,2,0:T(2,128)}, u32[]{:S(2)}) copy-start(f32[2,16,2]{1,2,0:T(2,128)} %param.13) | copy-start | bytes 772
  52.5 30.0 %copy-start.15 = (s32[1,4]{1,0:T(1,128)S(1)}, s32[1,4]{1,0:T(1,128)}, u32[]{:S(2)}) copy-start(s32[1,4]{1,0:T(1,128)} %param.11) | copy-start | bytes 52
  52.6 168.6 %all-gather.9.cloned.1.call-start = ((), (), s32[]{:S(2)}) async-start(), calls=%async_computation.4 | async-start | bytes 2359296 | tf_op jit(solution)/shard_map/all_gather | solution.py:205
  53.5 245.0 %all-gather.11.cloned.1.call-start = ((), (), s32[]{:S(2)}) async-start(), calls=%async_computation.5 | async-start | bytes 5013504 | tf_op jit(solution)/shard_map/all_gather | solution.py:205
  54.2 29.2 %copy-start.11 = (s32[1024]{0:T(1024)S(1)}, s32[1024]{0:T(1024)}, u32[]{:S(2)}) copy-start(s32[1024]{0:T(1024)} %param.12) | copy-start | bytes 12292
  81.1 1.3 copy-start.2
  85.5 16.3 %copy-start.6 = (pred[1024,1024]{0,1:T(8,128)(4,1)}, pred[1024,1024]{0,1:T(8,128)(4,1)S(1)}, u32[]{:S(2)}) copy-start(pred[1024,1024]{0,1:T(8,128)(4,1)S(1)} %get-tuple-element.61) | copy-start | bytes 3145732
  92.2 9.6 %copy-start.9 = (bf16[1024,256]{0,1:T(8,128)(2,1)S(1)}, bf16[1024,256]{0,1:T(8,128)(2,1)}, u32[]{:S(2)}) copy-start(bf16[1024,256]{0,1:T(8,128)(2,1)} %slice.326) | copy-start | bytes 1572868
  161.4 1.4 copy-start.3
  219.7 1.4 copy-start.4
  225.0 2.3 copy-start.7
  225.0 2.3 copy-start.8
  227.4 9.7 %copy-start.10 = (bf16[1024,4,32]{0,2,1:T(8,128)(2,1)S(1)}, bf16[1024,4,32]{0,2,1:T(8,128)(2,1)}, u32[]{:S(2)}) copy-start(bf16[1024,4,32]{0,2,1:T(8,128)(2,1)} %get-tuple-element.37) | copy-start | bytes 786436
  297.0 1.4 copy-start.5
  304.5 30.9 %copy-start.1 = (f32[256,1024]{1,0:T(8,128)S(1)}, f32[256,1024]{1,0:T(8,128)}, u32[]{:S(2)}) copy-start(f32[256,1024]{1,0:T(8,128)} %param.9) | copy-start | bytes 3145732
Sparse Core Ops, SparseCore 0:
  20.1 28.8 all-gather.4
  52.6 48.9 all-gather.6
  103.3 27.9 all-gather.8
  132.7 49.0 all-gather.10

commit v2 on v1

--- a/solution.py
+++ b/solution.py
@@ -132,24 +132,150 @@
         copy.wait_send()
 
 
+def square_kernel(reduce, gather, *refs):
+    refs = list(refs)
+    part = refs.pop(0) if reduce else None
+    residual = refs.pop(0)
+    gain = refs.pop(0) if gather else None
+    new_residual = refs.pop(0) if reduce else None
+    gathered = refs.pop(0) if gather else None
+    if reduce:
+        slots, onward, part_sent, part_got = refs[:4]
+        refs = refs[4:]
+    if gather:
+        held, norm_sent, norm_got = refs
+    rows, width = residual.shape
+    step = rows // CHUNKS
+    half = width // 2
+    front, back = pl.ds(0, half), pl.ds(half, half)
+    me = lax.axis_index("tp")
+    seq = lax.axis_index("seq")
+    major, minor = lax.div(me, 2), lax.rem(me, 2)
+    beside = major * 2 + (1 - minor)
+    above = (1 - major) * 2 + minor
+    across = (1 - major) * 2 + (1 - minor)
+
+    barrier = pltpu.get_barrier_semaphore()
+    for peer in (beside, above):
+        pl.semaphore_signal(barrier, inc=1, device_id=(seq, peer), device_id_type=MESH)
+    pl.semaphore_wait(barrier, 2)
+
+    def of(owner, c):
+        return pl.ds(pl.multiple_of(owner * rows + c * step, step), step)
+
+    started = []
+
+    def send(source, target, sent, got, peer):
+        copy = pltpu.make_async_remote_copy(
+            src_ref=source,
+            dst_ref=target,
+            send_sem=sent,
+            recv_sem=got,
+            device_id=(seq, peer),
+            device_id_type=MESH,
+        )
+        copy.start()
+        started.append(copy)
+        return copy
+
+    def send_part(kind, c, source, peer):
+        return send(source, slots.at[kind, c], part_sent.at[kind, c], part_got.at[kind, c], peer)
+
+    if reduce:
+        relay, own, passed = [], [], []
+        for c in range(CHUNKS):
+            relay.append(
+                (
+                    send_part(0, c, part.at[of(across, c), front], beside),
+                    send_part(1, c, part.at[of(across, c), back], above),
+                )
+            )
+        for c in range(CHUNKS):
+            own.append(
+                (
+                    send_part(2, c, part.at[of(beside, c), front], beside),
+                    send_part(3, c, part.at[of(above, c), back], above),
+                )
+            )
+        for c in range(CHUNKS):
+            pair = []
+            for side, columns, owner in ((0, front, above), (1, back, beside)):
+                relay[c][side].wait_recv()
+                onward[side, c] = (
+                    part[of(owner, c), columns].astype(jnp.float32)
+                    + slots[side, c].astype(jnp.float32)
+                ).astype(jnp.bfloat16)
+                pair.append(send_part(4 + side, c, onward.at[side, c], owner))
+            passed.append(pair)
+    whole = []
+    for c in range(CHUNKS):
+        here = pl.ds(c * step, step)
+        if reduce:
+            for side, columns in ((0, front), (1, back)):
+                own[c][side].wait_recv()
+                passed[c][side].wait_recv()
+                new_residual[here, columns] = residual[here, columns] + (
+                    part[of(me, c), columns].astype(jnp.float32)
+                    + slots[2 + side, c].astype(jnp.float32)
+                    + slots[4 + side, c].astype(jnp.float32)
+                )
+        if gather:
+            values = new_residual[here] if reduce else residual[here]
+            mine = held.at[of(me, c)]
+            held[of(me, c)] = rms_scaled(values, gain[...]).astype(jnp.bfloat16)
+            whole.append(
+                (
+                    send(mine, mine, norm_sent.at[0, c], norm_got.at[0, c], beside),
+                    send(mine, mine, norm_sent.at[1, c], norm_got.at[1, c], above),
+                )
+            )
+    if gather:
+        halves = []
+        for c in range(CHUNKS):
+            for side, columns, source, peer in (
+                (0, front, beside, above),
+                (1, back, above, beside),
+            ):
+                whole[c][side].wait_recv()
+                piece = held.at[of(source, c), columns]
+                halves.append(
+                    send(piece, piece, norm_sent.at[2 + side, c], norm_got.at[2 + side, c], peer)
+                )
+        for copy in halves:
+            copy.wait_recv()
+        gathered[...] = held[...]
+    for copy in started:
+        copy.wait_send()
+
+
 def exchange(n, residual, part=None, gain=None):
     reduce, gather = part is not None, gain is not None
     rows, width = residual.shape
     args = [residual]
     outs, scratch = [], []
-    copies = pltpu.SemaphoreType.DMA((CHUNKS, n - 1))
+    square = n == 4
+    part_copies = pltpu.SemaphoreType.DMA((6, CHUNKS) if square else (CHUNKS, n - 1))
+    norm_copies = pltpu.SemaphoreType.DMA((4, CHUNKS) if square else (CHUNKS, n - 1))
     if reduce:
         args = [part] + args
         outs.append(jax.ShapeDtypeStruct((rows, width), jnp.float32))
-        scratch += [pltpu.VMEM((CHUNKS, n - 1, rows // CHUNKS, width), jnp.bfloat16), copies, copies]
+        step = rows // CHUNKS
+        if square:
+            scratch.append(pltpu.VMEM((6, CHUNKS, step, width // 2), jnp.bfloat16))
+            scratch.append(pltpu.VMEM((2, CHUNKS, step, width // 2), jnp.bfloat16))
+        else:
+            scratch.append(pltpu.VMEM((CHUNKS, n - 1, step, width), jnp.bfloat16))
+        scratch += [part_copies, part_copies]
     if gather:
         args.append(gain)
         outs.append(jax.ShapeDtypeStruct((n * rows, width), jnp.bfloat16))
-        scratch += [pltpu.VMEM((n * rows, width), jnp.bfloat16), copies, copies]
+        scratch += [pltpu.VMEM((n * rows, width), jnp.bfloat16), norm_copies, norm_copies]
     vmem = pl.BlockSpec(memory_space=pltpu.VMEM)
     sides = int(reduce) + int(gather)
     return pl.pallas_call(
-        functools.partial(exchange_kernel, n, reduce, gather),
+        functools.partial(square_kernel, reduce, gather)
+        if square
+        else functools.partial(exchange_kernel, n, reduce, gather),
         out_shape=outs,
         in_specs=[vmem] * len(args),
         out_specs=[vmem] * len(outs),

time: 346 us -> 283 us (0.82)
  Pallas kernels: 189 us -> 127 us
    pallas_call x5, Pallas kernels: 189 us -> 127 us  [exchange(): pl.pallas_call(functools.partial(square_kernel, reduce, gather) if square...]
  transfers between devices with their start and end apart: 4 -> 4, of which waited for: 0 -> 0; matrix products, arithmetic and copies ran while one was open for 26% -> 31% of each run, Pallas kernels for 48% -> 41%
where the time goes in v2:
time: 283 us; the launch traced here: 280 us
  Pallas kernels  127 us (45%)
  matrix products  78.2 us (28%)
  blocking collectives  29.7 us (10%)
  local copies, waits for them, and re-layouts  22.4 us (8%)
  between operations  13.8 us (5%)
  other arithmetic  7.85 us (3%)
    pallas_call x5, Pallas kernels, exchange(): pl.pallas_call(functools.partial(square_kernel, reduce, gather) if square...  127 us
    all_to_all x2, blocking collectives, swap(): lax.all_to_all(jnp.concatenate(pieces, axis=2), 'tp', split_axis=0, conca...  29.7 us
    dot_general x2, matrix products, on_device(): jnp.einsum('hqk,khd->qhd', attn_weights, values, preferred_element_type=j...  21.4 us
    sub x2, matrix products, on_device(): weights_exp = jnp.exp(scores - row_peak)  19.3 us
    dot_general x2, matrix products, gated_units(): gate_up = jnp.dot(row_piece, weight, preferred_element_type=jnp.float32)  12.1 us
    dot_general x4, matrix products, project_out(): lax.dot_general(source, weight, (((1,), (1,)), ((), ())), preferred_eleme...  10.5 us
    dot_general x2, matrix products, project_rows(): return jnp.dot(row_piece, weight, preferred_element_type=jnp.float32)  8.19 us
    convert_element_type x14, local copies, waits for them, and re-layouts, by_owner(): trainer_rows[layer, :, starts[i]:starts[i] + widths[i]].astype(jnp.bfloat16)  6.75 us
  transfers between devices with their start and end apart: 4, of which 0 were waited for; matrix products, arithmetic and copies ran while one was open for 31% of the time, Pallas kernels for 41%

profile of v2, /device:TPU:0, one launch (start us, length us, event | category | flops | bytes accessed | tf_op | source)
XLA Modules:
  0.0 279.9 jit_solution(4637172360551920555)
XLA Ops:
  6.5 2.2 convert.46
  8.7 0.1 fusion.81
  8.9 0.1 pad_maximum_fusion.4
  9.1 0.1 copy.25
  9.1 10.8 %all_to_all.8 = bf16[4,32,1024]{2,1,0:T(8,128)(2,1)} all-to-all(bf16[4,32,1024]{2,1,0:T(8,128)(2,1)S(1)} %copy.25), channel_id=1, replica_groups=mesh['seq'=8,'tp'=4] {'tp'}, dimensions={0} | all-to-all | bytes 524288 | tf_op jit(solution)/shard_map/all_to_all | solution.py:325
  19.9 0.0 all-gather.5.cloned.1.call-update
  20.0 0.0 all-gather.7.cloned.1.call-start
  20.0 0.7 convert_element_type.146
  20.7 0.6 convert_element_type.147
  21.3 0.7 convert_element_type.148
  22.0 0.7 convert_element_type.149
  22.6 0.8 fusion.82
  23.5 1.2 convert_element_type.143
  24.6 0.2 convert_element_type.144
  24.9 0.2 convert_element_type.145
  25.1 0.2 convert_element_type.150
  25.4 1.2 convert_element_type.151
  26.6 0.9 convert_element_type.152
  27.5 4.7 %concatenate.25 = bf16[4,32,5248]{2,0,1:T(4,128)(2,1)S(1)} concatenate(bf16[4,32,704]{2,0,1:T(4,128)(2,1)S(1)} %bitcast.69, bf16[4,32,704]{2,0,1:T(4,128)(2,1)S(1)} %bitcast.70, bf16[4,32,704]{2,0,1:T(4,128)(2,1)S(1)} %bitcast.71, bf16[4,32,256]{2,0,1:T(4,128)(2,1)} %bitcast.79, bf16[4,32,256]{2,0,1:T(4,128)(2,1)} %bitcast.80, bf16[4,32,256]{2,0,1:T(4,128)(2,1)} %bitcast.81, ...), dimensions={2} | concatenate | bytes 2686976 | tf_op jit(solution)/shard_map/concatenate | solution.py:326
  32.2 0.1 copy.27
  32.4 18.9 %all_to_all.9 = bf16[4,32,5248]{2,1,0:T(8,128)(2,1)S(1)} all-to-all(bf16[4,32,5248]{2,1,0:T(8,128)(2,1)S(1)} %copy.27), channel_id=1, replica_groups=mesh['seq'=8,'tp'=4] {'tp'}, dimensions={0} | all-to-all | bytes 2686976 | tf_op jit(solution)/shard_map/all_to_all | solution.py:325
  51.3 1.2 fusion.83
  52.6 0.0 all-gather.9.cloned.1.call-start
  52.6 0.8 slice.259
  53.5 0.6 all-gather.11.cloned.1.call-start
  54.1 0.1 iota_add_fusion
  54.1 0.1 add.51
  54.3 1.4 fusion.45
  55.7 2.1 fusion.42.refs_0_.refs_1_
  57.8 18.3 %shard_map.73 = bf16[1024,1024]{1,0:T(8,128)(2,1)S(1)} custom-call(f32[256,1024]{1,0:T(8,128)S(1)} %fusion.42.refs_0_.refs_1_, f32[1,1024]{1,0:T(1,128)S(1)} %get-tuple-element.52.refs_1_), custom_call_target="tpu_custom_call" | custom-call | flops 2621440 | bytes 67108864 | tf_op jit(solution)/shard_map/pallas_call | solution.py:275
  76.1 1.3 copy-done.2
  77.4 0.1 dynamic-slice_bitcast_fusion
  77.5 0.1 select_reduce_fusion.1
  77.6 0.1 convert_reduce_fusion
  77.7 0.1 select_reduce_fusion
  77.9 0.5 multiply_cosine_fusion
  78.4 0.0 all-gather.11.cloned.1.call-update
  78.4 2.0 broadcast_compare_fusion
  80.5 4.3 %fusion.38 = f32[1024,768]{0,1:T(8,128)S(1)} fusion(bf16[1024,1024]{1,0:T(8,128)(2,1)} %copy-done.2, bf16[1024,1024]{1,0:T(8,128)(2,1)} %all-gather.5.cloned.1.call-done), kind=kOutput, calls=%fused_computation.51 | convolution fusion | flops 1610612736 | bytes 6815744 | tf_op jit(solution)/shard_map/dot_general | solution.py:47
  84.8 0.9 slice.326
  85.7 0.1 fusion.80
  85.8 1.3 subtract_convert_fusion.3
  87.1 9.6 %fusion.85 = f32[4,1024]{1,0:T(4,128)S(1)} fusion(f32[4]{0:T(128)S(1)} %get-tuple-element.60, f32[4]{0:T(128)S(1)} %get-tuple-element.59, pred[1024,1024]{0,1:T(8,128)(4,1)S(1)} %get-tuple-element.61, pred[1024,1024]{0,1:T(8,128)(4,1)} %get-tuple-element.62, bf16[1024,4,32]{0,2,1:T(8,128)(2,1)} %get-tuple-element.47, ...), kind=kOutput, calls=%fused_computation.120 | convolution fusion | flops 564134912 | bytes 3162144 | tf_op jit(solution)/shard_map/sub | solution.py:398
  96.8 10.5 %fusion.44 = bf16[4,64,1024]{2,1,0:T(8,128)(2,1)S(1)} fusion(bf16[1024,4,64]{0,2,1:T(8,128)(2,1)S(1)} %bitcast.76, f32[4,1024]{1,0:T(4,128)S(1)} %fusion.85, f32[4]{0:T(128)S(1)} %get-tuple-element.60, f32[4]{0:T(128)S(1)} %get-tuple-element.59, pred[1024,1024]{0,1:T(8,128)(4,1)S(1)} %get-tuple-element.61, pred[1024,1024]{0,1:T(8,128)(4,1)} %get-tuple-element.62, ...), kind=kOutput, calls=%fused_computation.55 | convolution fusion | flops 1105466368 | bytes 4210720 | tf_op jit(solution)/shard_map/hqk,khd->qhd/dot_general | solution.py:403
  107.2 1.8 convolution_convert_fusion.1.refs_0_
  109.0 33.7 %shard_map.74 = (f32[256,1024]{1,0:T(8,128)S(1)}, bf16[1024,1024]{1,0:T(8,128)(2,1)S(1)}) custom-call(bf16[1024,1024]{1,0:T(8,128)(2,1)S(1)} %convolution_convert_fusion.1.refs_0_, f32[256,1024]{1,0:T(8,128)S(1)} %fusion.42.refs_0_.refs_1_, f32[1,1024]{1,0:T(1,128)S(1)} %get-tuple-element.51.refs_2_), custom_call_target="tpu_custom_call" | custom-call | flops 2621440 | bytes 134217728 | tf_op jit(solution)/shard_map/pallas_call | solution.py:275
  142.8 1.4 copy-done.3
  144.2 6.1 %fusion.25 = f32[1024,1408]{1,0:T(8,128)S(1)} fusion(bf16[1024,1024]{1,0:T(8,128)(2,1)} %copy-done.3, bf16[1024,2112]{1,0:T(8,128)(2,1)} %all-gather.7.cloned.1.call-done), kind=kOutput, calls=%fused_computation.34 | convolution fusion | flops 2952790016 | bytes 10747904 | tf_op jit(solution)/shard_map/dot_general | solution.py:51
  150.3 3.3 %convolution_convert_fusion.3.refs_0_ = bf16[1024,1024]{1,0:T(8,128)(2,1)S(1)} fusion(bf16[1024,2112]{1,0:T(8,128)(2,1)} %all-gather.7.cloned.1.call-done, f32[1024,1408]{1,0:T(8,128)S(1)} %fusion.25), kind=kOutput, calls=%fused_computation.46 | convolution fusion | flops 1481768960 | bytes 9961472 | tf_op jit(solution)/shard_map/dot_general | solution.py:57
  153.6 32.0 %shard_map.75 = (f32[256,1024]{1,0:T(8,128)S(1)}, bf16[1024,1024]{1,0:T(8,128)(2,1)S(1)}) custom-call(bf16[1024,1024]{1,0:T(8,128)(2,1)S(1)} %convolution_convert_fusion.3.refs_0_, f32[256,1024]{1,0:T(8,128)S(1)} %get-tuple-element.12.refs_1_, f32[1,1024]{1,0:T(1,128)S(1)} %get-tuple-element.50.refs_2_), custom_call_target="tpu_custom_call" | custom-call | flops 2621440 | bytes 134217728 | tf_op jit(solution)/shard_map/pallas_call | solution.py:275
  185.6 1.4 copy-done.4
  186.9 3.9 %fusion.35 = f32[1024,768]{0,1:T(8,128)S(1)} fusion(bf16[1024,1024]{1,0:T(8,128)(2,1)} %copy-done.4, bf16[1024,1024]{1,0:T(8,128)(2,1)} %all-gather.9.cloned.1.call-done), kind=kOutput, calls=%fused_computation.48 | convolution fusion | flops 1610612736 | bytes 6815744 | tf_op jit(solution)/shard_map/dot_general | solution.py:47
  190.9 0.9 slice.325
  191.8 0.1 fusion.79
  191.9 1.3 subtract_convert_fusion.1
  193.2 9.7 %fusion.86 = f32[4,1024]{1,0:T(4,128)S(1)} fusion(f32[4]{0:T(128)S(1)} %get-tuple-element.58, f32[4]{0:T(128)S(1)} %get-tuple-element.57, pred[1024,1024]{0,1:T(8,128)(4,1)S(1)} %copy-done.7, pred[1024,1024]{0,1:T(8,128)(4,1)S(1)} %copy-done.8, bf16[1024,4,32]{0,2,1:T(8,128)(2,1)} %get-tuple-element.45, bf16[1024,4,32]{0,2,1:T(8,128)(2,1)} %get-tuple-element.46, ...), kind=kOutput, calls=%fused_computation.121 | convolution fusion | flops 564134912 | bytes 3162144 | tf_op jit(solution)/shard_map/sub | solution.py:398
  202.9 11.0 %fusion.43 = bf16[4,64,1024]{2,1,0:T(8,128)(2,1)} fusion(bf16[1024,4,64]{0,2,1:T(8,128)(2,1)} %bitcast.75, f32[4,1024]{1,0:T(4,128)S(1)} %fusion.86, f32[4]{0:T(128)S(1)} %get-tuple-element.58, f32[4]{0:T(128)S(1)} %get-tuple-element.57, pred[1024,1024]{0,1:T(8,128)(4,1)S(1)} %copy-done.7, pred[1024,1024]{0,1:T(8,128)(4,1)S(1)} %copy-done.8, ...), kind=kOutput, calls=%fused_computation.54 | convolution fusion | flops 1105466368 | bytes 4210720 | tf_op jit(solution)/shard_map/hqk,khd->qhd/dot_general | solution.py:403
  213.9 2.0 convolution_convert_fusion.refs_0_
  215.9 31.0 %shard_map.76 = (f32[256,1024]{1,0:T(8,128)S(1)}, bf16[1024,1024]{1,0:T(8,128)(2,1)S(1)}) custom-call(bf16[1024,1024]{1,0:T(8,128)(2,1)S(1)} %convolution_convert_fusion.refs_0_, f32[256,1024]{1,0:T(8,128)S(1)} %get-tuple-element.14.refs_1_, f32[1,1024]{1,0:T(1,128)S(1)} %get-tuple-element.49.refs_2_), custom_call_target="tpu_custom_call" | custom-call | flops 2621440 | bytes 134217728 | tf_op jit(solution)/shard_map/pallas_call | solution.py:275
  246.8 1.4 copy-done.5
  248.2 6.0 %fusion.23 = f32[1024,1408]{1,0:T(8,128)S(1)} fusion(bf16[1024,1024]{1,0:T(8,128)(2,1)} %copy-done.5, bf16[1024,2112]{1,0:T(8,128)(2,1)} %all-gather.11.cloned.1.call-done), kind=kOutput, calls=%fused_computation.32 | convolution fusion | flops 2952790016 | bytes 10747904 | tf_op jit(solution)/shard_map/dot_general | solution.py:51
  254.2 3.4 %convolution_convert_fusion.2.refs_0_ = bf16[1024,1024]{1,0:T(8,128)(2,1)S(1)} fusion(bf16[1024,2112]{1,0:T(8,128)(2,1)} %all-gather.11.cloned.1.call-done, f32[1024,1408]{1,0:T(8,128)S(1)} %fusion.23), kind=kOutput, calls=%fused_computation.45 | convolution fusion | flops 1481768960 | bytes 9961472 | tf_op jit(solution)/shard_map/dot_general | solution.py:57
  257.6 12.4 %shard_map.77 = f32[256,1024]{1,0:T(8,128)S(1)} custom-call(bf16[1024,1024]{1,0:T(8,128)(2,1)S(1)} %convolution_convert_fusion.2.refs_0_, f32[256,1024]{1,0:T(8,128)S(1)} %get-tuple-element.16.refs_1_), custom_call_target="tpu_custom_call" | custom-call | flops 2621440 | bytes 67108864 | tf_op jit(solution)/shard_map/pallas_call | solution.py:275
  270.1 3.2 %fusion.18 = f32[256,1024]{1,0:T(8,128)} fusion(f32[256,1024]{1,0:T(8,128)S(1)} %shard_map.77, s32[1024]{0:T(1024)S(1)} %add.51), kind=kOutput, calls=%fused_computation.25 | convolution fusion | flops 3222274048 | bytes 2101248 | tf_op jit(solution)/shard_map/dot_general | solution.py:297
  (47 shorter events, 0.3 us)
Async XLA Ops:
  6.5 49.1 %copy-start = (f32[256,1024]{1,0:T(8,128)S(1)}, f32[256,1024]{1,0:T(8,128)}, u32[]{:S(2)}) copy-start(f32[256,1024]{1,0:T(8,128)} %param.9) | copy-start | bytes 3145732
  6.5 73.9 %all-gather.5.cloned.1.call-start = ((), (), s32[]{:S(2)}) async-start(), calls=%async_computation.2 | async-start | bytes 2359296 | tf_op jit(solution)/shard_map/all_gather | solution.py:331
  20.0 124.2 %all-gather.7.cloned.1.call-start = ((), (), s32[]{:S(2)}) async-start(), calls=%async_computation.3 | async-start | bytes 5013504 | tf_op jit(solution)/shard_map/all_gather | solution.py:331
  32.2 21.8 %copy-start.14 = (s32[32]{0:T(128)S(1)}, s32[32]{0:T(128)}, u32[]{:S(2)}) copy-start(s32[32]{0:T(128)} %param.8) | copy-start | bytes 388
  32.2 22.0 %copy-start.12 = (f32[2,2,1024]{2,1,0:T(2,128)S(1)}, f32[2,2,1024]{2,1,0:T(2,128)}, u32[]{:S(2)}) copy-start(f32[2,2,1024]{2,1,0:T(2,128)} %param.10) | copy-start | bytes 49156
  52.5 24.9 %copy-start.13 = (f32[2,16,2]{1,2,0:T(2,128)S(1)}, f32[2,16,2]{1,2,0:T(2,128)}, u32[]{:S(2)}) copy-start(f32[2,16,2]{1,2,0:T(2,128)} %param.13) | copy-start | bytes 772
  52.5 25.0 %copy-start.15 = (s32[1,4]{1,0:T(1,128)S(1)}, s32[1,4]{1,0:T(1,128)}, u32[]{:S(2)}) copy-start(s32[1,4]{1,0:T(1,128)} %param.11) | copy-start | bytes 52
  52.6 134.4 %all-gather.9.cloned.1.call-start = ((), (), s32[]{:S(2)}) async-start(), calls=%async_computation.4 | async-start | bytes 2359296 | tf_op jit(solution)/shard_map/all_gather | solution.py:331
  53.5 194.7 %all-gather.11.cloned.1.call-start = ((), (), s32[]{:S(2)}) async-start(), calls=%async_computation.5 | async-start | bytes 5013504 | tf_op jit(solution)/shard_map/all_gather | solution.py:331
  54.2 24.2 %copy-start.11 = (s32[1024]{0:T(1024)S(1)}, s32[1024]{0:T(1024)}, u32[]{:S(2)}) copy-start(s32[1024]{0:T(1024)} %param.12) | copy-start | bytes 12292
  76.1 1.3 copy-start.2
  80.5 16.3 %copy-start.6 = (pred[1024,1024]{0,1:T(8,128)(4,1)}, pred[1024,1024]{0,1:T(8,128)(4,1)S(1)}, u32[]{:S(2)}) copy-start(pred[1024,1024]{0,1:T(8,128)(4,1)S(1)} %get-tuple-element.61) | copy-start | bytes 3145732
  87.1 9.6 %copy-start.9 = (bf16[1024,256]{0,1:T(8,128)(2,1)S(1)}, bf16[1024,256]{0,1:T(8,128)(2,1)}, u32[]{:S(2)}) copy-start(bf16[1024,256]{0,1:T(8,128)(2,1)} %slice.326) | copy-start | bytes 1572868
  142.8 1.4 copy-start.3
  185.6 1.4 copy-start.4
  190.9 2.3 copy-start.7
  190.9 2.3 copy-start.8
  193.2 9.7 %copy-start.10 = (bf16[1024,4,32]{0,2,1:T(8,128)(2,1)S(1)}, bf16[1024,4,32]{0,2,1:T(8,128)(2,1)}, u32[]{:S(2)}) copy-start(bf16[1024,4,32]{0,2,1:T(8,128)(2,1)} %get-tuple-element.37) | copy-start | bytes 786436
  246.8 1.4 copy-start.5
  254.2 19.0 %copy-start.1 = (f32[256,1024]{1,0:T(8,128)S(1)}, f32[256,1024]{1,0:T(8,128)}, u32[]{:S(2)}) copy-start(f32[256,1024]{1,0:T(8,128)} %param.9) | copy-start | bytes 3145732
Sparse Core Ops, SparseCore 0:
  20.1 28.8 all-gather.4
  52.6 48.9 all-gather.6
  103.3 27.9 all-gather.8
  132.7 49.0 all-gather.10
